TPU v7x, 32 devices: a whole 2x2x4 slice. The times are simulated.
32 devices in a mesh: coil: 2 (over x), ro: 16 (over z, y, core).
Axes of the slice: x: 2, y: 2, z: 4, core: 2. Of those that a mesh axis runs over, the one named last changes fastest.
Arguments:
- kspace: bfloat16 [2, 64, 16, 448, 320], P(None, 'coil', None, 'ro'), may hold values from -884272563206990856199 to 884272563206990856199
- sensitivity: bfloat16 [2, 64, 16, 448, 320], P(None, 'coil', 'ro'), may hold values from -0.75 to 0.75
- sampled: int32 [16, 448], replicated, may hold values 0 or 1
- pole_y: int32 [16, 320], replicated, may hold values from 4 to 112
- order_y: int32 [16, 320], replicated, may hold values from 1 to 3
- pole_z: int32 [16, 448], replicated, may hold values from 4 to 80
- order_z: int32 [16, 448], replicated, may hold values from 1 to 3
Outputs:
- image: float32 [2, 16, 448, 320], P(None, 'ro', 'coil')
All inputs are finite; a program needn't handle non-finite values.
Results may differ from a plain program's by a relative error of at most 0.0056.
Values may be sent and summed in bfloat16 or wider, within the bound.
No kernel may reach another device: no remote copies, remote signals or barrier semaphores. Data moves between devices by JAX's collectives and lax.ppermute only.
A program may use at most 192 MiB of HBM per device.

v0:
```python
import math

import jax
import jax.numpy as jnp
from jax import lax
from jax.sharding import PartitionSpec as P


def dft_tables(length):
    index = jnp.arange(length, dtype=jnp.int32)
    product = index[:, None] * index[None, :] % length
    angle = product.astype(jnp.float32) * (2.0 * math.pi / length)
    factor = 1.0 / math.sqrt(length)
    return (
        (jnp.cos(angle) * factor).astype(jnp.bfloat16),
        (jnp.sin(angle) * factor).astype(jnp.bfloat16),
    )


def line_window(frequency, pole, degree):
    quotient = frequency / pole.astype(jnp.float32)
    return 1.0 / (1.0 + jnp.power(quotient, 2.0 * degree.astype(jnp.float32)))


def kz_transform(filtered, kz_cosine, kz_sine):
    real_part, imag_part = (filtered[0], filtered[1])
    hyb_real = jnp.einsum(
        "cakz,zn->cakn", real_part, kz_cosine, preferred_element_type=jnp.float32
    ) - jnp.einsum("cakz,zn->cakn", imag_part, kz_sine, preferred_element_type=jnp.float32)
    hyb_imag = jnp.einsum(
        "cakz,zn->cakn", real_part, kz_sine, preferred_element_type=jnp.float32
    ) + jnp.einsum("cakz,zn->cakn", imag_part, kz_cosine, preferred_element_type=jnp.float32)
    return jnp.stack([hyb_real, hyb_imag]).astype(jnp.bfloat16)


def on_device(kspace, sensitivity, sampled, pole_y, order_y, pole_z, order_z):
    lines_local = kspace.shape[3]
    kz_count = kspace.shape[4]
    ky_count = lines_local * lax.axis_size("ro")
    first_line = lax.axis_index("ro") * lines_local
    kz_cosine, kz_sine = dft_tables(kz_count)
    ky_cosine, ky_sine = dft_tables(ky_count)
    line_index = first_line + jnp.arange(lines_local, dtype=jnp.int32)
    freq_y = jnp.minimum(line_index, ky_count - line_index).astype(jnp.float32)
    col_index = jnp.arange(kz_count, dtype=jnp.int32)
    freq_z = jnp.minimum(col_index, kz_count - col_index).astype(jnp.float32)
    local_sampled = lax.dynamic_slice_in_dim(sampled, first_line, lines_local, 1)
    local_pole_z = lax.dynamic_slice_in_dim(pole_z, first_line, lines_local, 1)
    local_order_z = lax.dynamic_slice_in_dim(order_z, first_line, lines_local, 1)
    weight_y = local_sampled[:, :, None].astype(jnp.float32) * line_window(
        freq_y[None, :, None], pole_y[:, None, :], order_y[:, None, :]
    )
    weight_z = line_window(
        freq_z[None, None, :], local_pole_z[:, :, None], local_order_z[:, :, None]
    )
    filtered = (kspace.astype(jnp.float32) * (weight_y * weight_z)).astype(jnp.bfloat16)
    arrived = lax.all_to_all(filtered, "ro", split_axis=2, concat_axis=3, tiled=True)
    moved = kz_transform(arrived, kz_cosine, kz_sine)
    hyb_real, hyb_imag = (moved[0], moved[1])
    img_real = jnp.einsum(
        "nk,cakz->canz", ky_cosine, hyb_real, preferred_element_type=jnp.float32
    ) - jnp.einsum("nk,cakz->canz", ky_sine, hyb_imag, preferred_element_type=jnp.float32)
    img_imag = jnp.einsum(
        "nk,cakz->canz", ky_sine, hyb_real, preferred_element_type=jnp.float32
    ) + jnp.einsum("nk,cakz->canz", ky_cosine, hyb_imag, preferred_element_type=jnp.float32)
    map_real = sensitivity[0]
    map_imag = sensitivity[1]
    out_real = jnp.sum(map_real * img_real + map_imag * img_imag, axis=0)
    out_imag = jnp.sum(map_real * img_imag - map_imag * img_real, axis=0)
    partial_image = jnp.stack([out_real, out_imag])
    return lax.psum_scatter(partial_image, "coil", scatter_dimension=2, tiled=True)


def solution(mesh):
    return jax.shard_map(
        on_device,
        mesh=mesh,
        in_specs=(
            P(None, "coil", None, "ro", None),
            P(None, "coil", "ro", None, None),
            P(),
            P(),
            P(),
            P(),
            P(),
        ),
        out_specs=P(None, "ro", "coil", None),
        check_vma=False,
    )
```

profile of v0, /device:TPU:0, one launch (start us, length us, event | category | flops | bytes accessed | tf_op | source)
XLA Modules:
  0.0 749.0 jit_solution(12215638042570538222)
XLA Ops:
  6.5 0.7 convert_element_type.122
  7.3 0.7 convert_multiply_fusion.4
  8.0 0.8 convert_multiply_fusion.5
  8.8 0.8 dynamic-slice_convert_fusion
  9.6 2.5 fusion.11
  12.1 17.3 %multiply_convert_fusion = bf16[2,32,16,28,320]{4,1,3,0,2:T(8,128)(2,1)} fusion(bf16[2,32,16,28,320]{4,2,3,1,0:T(8,128)(2,1)} %param.7, f32[16,28,320]{2,1,0:T(8,128)S(1)} %fusion.11), kind=kLoop, calls=%fused_computation | loop fusion | flops 27525120 | bytes 37273600 | tf_op jit(solution)/shard_map/convert_element_type | solution.py:56
  29.4 7.4 all-to-all-start
  36.8 0.3 reduce-scatter.4.cloned.1.call-start
  37.2 3.7 fusion.23.clone.4
  40.9 384.0 %all-to-all-done = bf16[2,32,16,28,320]{4,1,3,0,2:T(8,128)(2,1)} async-done(((bf16[2,32,16,28,320]{4,1,3,0,2:T(8,128)(2,1)}), bf16[2,32,16,28,320]{4,1,3,0,2:T(8,128)(2,1)}, u32[]{:S(2)}, u32[]{:S(2)}) %all-to-all-start) | async-done | bytes 18350112 | tf_op jit(solution)/shard_map/all_to_all | solution.py:57
  424.9 17.1 %fusion.72 = (bf16[1,32,16,28,320]{4,1,3,0,2:T(8,128)(2,1)}, bf16[1,32,16,28,320]{4,1,3,0,2:T(8,128)(2,1)}) fusion(bf16[2,32,16,28,320]{4,1,3,0,2:T(8,128)(2,1)} %all-to-all-done), kind=kLoop, calls=%fused_computation.91 | loop fusion | bytes 36700160 | tf_op jit(solution)/shard_map/slice | solution.py:26
  442.0 15.9 %copy.37 = bf16[32,448,320]{1,2,0:T(8,128)(2,1)} copy(bf16[32,448,320]{2,0,1:T(8,128)(2,1)} %bitcast.118) | data formatting | bytes 18350080 | tf_op jit(solution)/shard_map/reshape.4
  457.9 0.0 copy-start
  457.9 15.6 %fusion.35 = f32[32,448,320]{1,2,0:T(8,128)} fusion(bf16[32,448,320]{1,2,0:T(8,128)(2,1)} %copy.37), kind=kOutput, calls=%fused_computation.50 | convolution fusion | flops 2937139200 | bytes 27525120 | tf_op jit(solution)/shard_map/cakz,zn->cakn/dot_general | solution.py:27
  473.5 0.0 copy-done
  473.5 11.4 %fusion.33 = f32[32,448,320]{1,2,0:T(8,128)} fusion(bf16[32,448,320]{1,2,0:T(8,128)(2,1)S(1)} %copy-done), kind=kOutput, calls=%fused_computation.49 | convolution fusion | flops 2937139200 | bytes 27525120 | tf_op jit(solution)/shard_map/cakz,zn->cakn/dot_general | solution.py:30
  484.9 15.8 %copy.38 = bf16[32,448,320]{1,2,0:T(8,128)(2,1)} copy(bf16[32,448,320]{2,0,1:T(8,128)(2,1)} %bitcast.117) | data formatting | bytes 18350080 | tf_op jit(solution)/shard_map/reshape.9
  500.7 17.4 %add_convert_fusion = bf16[32,448,320]{1,2,0:T(8,128)(2,1)} fusion(f32[32,448,320]{1,2,0:T(8,128)} %fusion.33, bf16[32,448,320]{1,2,0:T(8,128)(2,1)} %copy.38), kind=kOutput, calls=%fused_computation.9 | convolution fusion | flops 2946314240 | bytes 36700160 | tf_op jit(solution)/shard_map/cakz,zn->cakn/dot_general | solution.py:32
  518.1 18.5 %fusion.26 = f32[32,320,448]{2,1,0:T(8,128)} fusion(bf16[32,448,320]{1,2,0:T(8,128)(2,1)} %add_convert_fusion), kind=kOutput, calls=%fused_computation.45 | convolution fusion | flops 4112625664 | bytes 27525120 | tf_op jit(solution)/shard_map/nk,cakz->canz/dot_general | solution.py:65
  536.6 18.7 %fusion.24 = f32[32,320,448]{2,1,0:T(8,128)} fusion(bf16[32,448,320]{1,2,0:T(8,128)(2,1)} %add_convert_fusion), kind=kOutput, calls=%fused_computation.44 | convolution fusion | flops 4112625664 | bytes 27525120 | tf_op jit(solution)/shard_map/nk,cakz->canz/dot_general | solution.py:62
  555.3 17.0 %subtract_convert_fusion = bf16[32,448,320]{1,2,0:T(8,128)(2,1)} fusion(f32[32,448,320]{1,2,0:T(8,128)} %fusion.35, bf16[32,448,320]{1,2,0:T(8,128)(2,1)} %copy.38), kind=kOutput, calls=%fused_computation.10 | convolution fusion | flops 2946314240 | bytes 36700160 | tf_op jit(solution)/shard_map/cakz,zn->cakn/dot_general | solution.py:29
  572.3 18.5 %fusion.28 = f32[32,320,448]{2,1,0:T(8,128)} fusion(bf16[32,448,320]{1,2,0:T(8,128)(2,1)} %subtract_convert_fusion), kind=kOutput, calls=%fused_computation.46 | convolution fusion | flops 4112625664 | bytes 27525120 | tf_op jit(solution)/shard_map/nk,cakz->canz/dot_general | solution.py:60
  590.8 31.5 %fusion.1 = (f32[448,320]{0,1:T(8,128)S(1)}, f32[448,320]{0,1:T(8,128)S(1)}) fusion(bf16[2,32,1,448,320]{3,4,1,2,0:T(8,128)(2,1)} %bitcast.119, f32[32,320,448]{2,1,0:T(8,128)} %fusion.26, f32[32,320,448]{2,1,0:T(8,128)} %fusion.28, f32[32,320,448]{2,1,0:T(8,128)} %fusion.24, bf16[32,448,320]{1,2,0:T(8,128)(2,1)} %subtract_convert_fusion, ...), kind=kOutput, calls=%fused_computation.6 | convolution fusion | flops 4165181440 | bytes 84123648 | tf_op jit(solution)/shard_map/nk,cakz->canz/dot_general | solution.py:63
  622.3 0.1 pad_maximum_fusion
  622.4 2.0 copy.42
  624.4 4.3 bitcast_reduce_fusion
  628.7 1.9 reshape.159
  630.6 0.0 reduce-scatter.4.cloned.1.call-update
  630.6 108.1 %reduce-scatter.4.cloned.1.call-done = f32[224,640]{1,0:T(8,128)} async-done(((f32[448,640]{1,0:T(8,128)}), f32[224,640]{1,0:T(8,128)}) %reduce-scatter.4.cloned.1.call-update) | async-done | bytes 573456
  738.7 1.9 reshape.160
  740.6 1.2 copy.43
  (2 shorter events, 0.0 us)
Async XLA Ops:
  29.4 395.5 %all-to-all-start = ((bf16[2,32,16,28,320]{4,1,3,0,2:T(8,128)(2,1)}), bf16[2,32,16,28,320]{4,1,3,0,2:T(8,128)(2,1)}, u32[]{:S(2)}, u32[]{:S(2)}) async-start(bf16[2,32,16,28,320]{4,1,3,0,2:T(8,128)(2,1)} %multiply_convert_fusion), calls=%async_computation | async-start | bytes 44040192 | tf_op jit(solution)/shard_map/all_to_all | solution.py:57
  36.8 701.9 %reduce-scatter.4.cloned.1.call-start = ((), (), s32[]{:S(2)}) async-start(), calls=%async_computation.2 | async-start | bytes 1720320
  457.9 15.6 %copy-start = (bf16[32,448,320]{1,2,0:T(8,128)(2,1)S(1)}, bf16[32,448,320]{1,2,0:T(8,128)(2,1)}, u32[]{:S(2)}) copy-start(bf16[32,448,320]{1,2,0:T(8,128)(2,1)} %copy.37) | copy-start | bytes 27525124
Sparse Core Ops, SparseCore 0:
  630.7 107.9 reduce-scatter.3
where the time goes:
time: 754 us; the launch traced here: 749 us
  waiting for transfers between devices  492 us (65%)
  matrix products  149 us (20%)
  local copies, waits for them, and re-layouts  60.2 us (8%)
  other arithmetic  26.7 us (4%)
  between operations  13.8 us (2%)
  starting transfers between devices  7.72 us (1%)
    all_to_all x1, waiting for transfers between devices, on_device(): lax.all_to_all(filtered, 'ro', split_axis=2, concat_axis=3, tiled=True)  384 us
    unnamed x2, waiting for transfers between devices  108 us
    another operation x2, local copies, waits for them, and re-layouts  31.7 us
    dot_general x1, matrix products, on_device(): jnp.einsum('nk,cakz->canz', ky_sine, hyb_real, preferred_element_type=jnp...  31.5 us
    dot_general x1, matrix products, on_device(): jnp.einsum('nk,cakz->canz', ky_sine, hyb_imag, preferred_element_type=jnp...  18.7 us
    dot_general x1, matrix products, on_device(): jnp.einsum('nk,cakz->canz', ky_cosine, hyb_real, preferred_element_type=j...  18.5 us
    dot_general x1, matrix products, on_device(): jnp.einsum('nk,cakz->canz', ky_cosine, hyb_imag, preferred_element_type=j...  18.5 us
    dot_general x1, matrix products, kz_transform(): jnp.einsum('cakz,zn->cakn', imag_part, kz_cosine, preferred_element_type=...  17.4 us
  transfers between devices with their start and end apart: 2, of which 2 were waited for; matrix products, arithmetic and copies ran while one was open for 0% of the time, Pallas kernels for 0%

commit v1 on v0

v1 whole, which is shorter than its diff:
```python
import functools
import math

import jax
import jax.numpy as jnp
import ml_dtypes
import numpy as np
from jax import lax
from jax.experimental import pallas as pl
from jax.experimental.pallas import tpu as pltpu
from jax.sharding import PartitionSpec as P

LANES = 128
VMEM_BYTES = 56 * 2**20
PLAN = (3, 4, 1)


def round_up(value, step):
    return (value + step - 1) // step * step


def dft_tables(length):
    index = np.arange(length, dtype=np.int64)
    product = index[:, None] * index[None, :] % length
    angle = product.astype(np.float32) * np.float32(2.0 * math.pi / length)
    factor = np.float32(1.0 / math.sqrt(length))
    return (
        (np.cos(angle) * factor).astype(ml_dtypes.bfloat16).astype(np.float32),
        (np.sin(angle) * factor).astype(ml_dtypes.bfloat16).astype(np.float32),
    )


def kz_table(length, half):
    cosine, sine = dft_tables(length)
    table = np.zeros((2 * length, 2 * half), np.float32)
    table[:length, :length] = cosine
    table[length:, :length] = -sine
    table[:length, half : half + length] = sine
    table[length:, half : half + length] = cosine
    return jnp.asarray(table.astype(ml_dtypes.bfloat16))


def ky_table(length, groups, stride):
    lines = length // groups
    parts = []
    for part in dft_tables(length):
        padded = np.zeros((length, groups, stride), np.float32)
        padded[:, :, :lines] = part.reshape(length, groups, lines)
        parts.append(padded.reshape(length, groups * stride))
    return jnp.asarray(np.concatenate(parts, axis=1).astype(ml_dtypes.bfloat16))


def growth(frequency, pole, order):
    quotient = frequency / pole
    square = quotient * quotient
    fourth = square * square
    return 1.0 + jnp.where(order < 1.5, square, jnp.where(order < 2.5, fourth, fourth * square))


def fold(index, length):
    return jnp.minimum(index, length - index).astype(jnp.float32)


def filter_kernel(
    readouts, group, lines, first_ref, x_ref, sampled_ref, pole_y_ref, order_y_ref, pole_z_ref, order_z_ref, o_ref, weight, packed
):
    kz_count = x_ref.shape[-1]
    ky_count = sampled_ref.shape[-1]

    @pl.when(pl.program_id(0) == 0)
    def _():
        first = first_ref[0]
        rows = round_up(lines, 8)
        line = lax.broadcasted_iota(jnp.int32, (rows, ky_count), 0) + first
        place = lax.broadcasted_iota(jnp.int32, (rows, ky_count), 1)
        pick = (line == place).astype(jnp.bfloat16)

        def mine(ref):
            return lax.dot_general(
                pick,
                ref[...].astype(jnp.float32).astype(jnp.bfloat16),
                (((1,), (1,)), ((), ())),
                preferred_element_type=jnp.float32,
            )

        sampled, pole_z, order_z = mine(sampled_ref), mine(pole_z_ref), mine(order_z_ref)
        freq_y = fold(lax.broadcasted_iota(jnp.int32, (rows, kz_count), 0) + first, ky_count)
        freq_z = fold(lax.broadcasted_iota(jnp.int32, (rows, kz_count), 1), kz_count)
        for r in range(readouts):
            column_y = growth(
                freq_y, pole_y_ref[r : r + 1, :].astype(jnp.float32), order_y_ref[r : r + 1, :].astype(jnp.float32)
            )
            column_z = growth(freq_z, pole_z[:, r : r + 1], order_z[:, r : r + 1])
            weight[r] = (sampled[:, r : r + 1] / (column_y * column_z))[:lines]

    def one(r, _):
        w = weight[r]
        for c in range(group):
            for part in range(2):
                packed[pl.ds(lines * c, lines), pl.ds(part * kz_count, kz_count)] = (
                    x_ref[part, c, r].astype(jnp.float32) * w
                )
        o_ref[r] = packed[...].astype(jnp.bfloat16)
        return 0

    lax.fori_loop(0, readouts, one, 0)


def filter_chunk(kspace, first_line, params, group, first_unit, units):
    _, _, readouts, lines, kz_count = kspace.shape
    rows = group * lines
    whole = [pl.BlockSpec(p.shape, lambda i, first: (0, 0)) for p in params]
    return pl.pallas_call(
        functools.partial(filter_kernel, readouts, group, lines),
        out_shape=jax.ShapeDtypeStruct((readouts, units * rows, 2 * kz_count), jnp.bfloat16),
        grid_spec=pltpu.PrefetchScalarGridSpec(
            num_scalar_prefetch=1,
            grid=(units,),
            in_specs=[
                pl.BlockSpec((2, group, readouts, lines, kz_count), lambda i, first: (0, i + first_unit, 0, 0, 0)),
                *whole,
            ],
            out_specs=pl.BlockSpec((readouts, rows, 2 * kz_count), lambda i, first: (0, i, 0)),
            scratch_shapes=[
                pltpu.VMEM((readouts, lines, kz_count), jnp.float32),
                pltpu.VMEM((rows, 2 * kz_count), jnp.float32),
            ],
        ),
        compiler_params=pltpu.CompilerParams(vmem_limit_bytes=VMEM_BYTES),
        cost_estimate=pl.CostEstimate(
            flops=0, bytes_accessed=5 * units * readouts * rows * 2 * kz_count, transcendentals=0
        ),
        name="window_lines",
    )(first_line, kspace, *params)


def image_kernel(group, lines, stride, fresh, last, halves, me_ref, x_ref, maps_ref, kz_ref, ky_ref, *refs):
    refs = list(refs)
    acc_in = None if fresh else refs.pop(0)
    outs, (wide, hybrid, acc) = refs[:-3], refs[-3:]
    sources, rows, packed = x_ref.shape
    ky_count, kz_count = maps_ref.shape[-2:]
    half = kz_ref.shape[1] // 2
    depth = sources * stride
    step = pl.program_id(0)

    @pl.when(step == 0)
    def _():
        acc[...] = jnp.zeros_like(acc) if fresh else acc_in[...]
        hybrid[...] = jnp.zeros_like(hybrid)

    wide[...] = jnp.dot(
        x_ref[...].reshape(sources * rows, packed), kz_ref[...], preferred_element_type=jnp.float32
    ).reshape(sources, rows, 2 * half)

    def place(s, _):
        base = pl.multiple_of(s * stride, stride)
        for c in range(group):
            block = wide[s, pl.ds(lines * c, lines), :]
            real, imag = block[:, :half], block[:, half:]
            hybrid[c, pl.ds(base, lines), :half] = real.astype(jnp.bfloat16)
            hybrid[c, pl.ds(base, lines), half:] = imag.astype(jnp.bfloat16)
            hybrid[c, pl.ds(depth + base, lines), :half] = (-imag).astype(jnp.bfloat16)
            hybrid[c, pl.ds(depth + base, lines), half:] = real.astype(jnp.bfloat16)
        return 0

    lax.fori_loop(0, sources, place, 0)

    def one(c, _):
        image = jnp.dot(ky_ref[...], hybrid[c], preferred_element_type=jnp.float32)
        real, imag = image[:, :kz_count], image[:, half : half + kz_count]
        map_real = maps_ref[0, c, 0].astype(jnp.float32)
        map_imag = maps_ref[1, c, 0].astype(jnp.float32)
        acc[0] += map_real * real + map_imag * imag
        acc[1] += map_real * imag - map_imag * real
        return 0

    lax.fori_loop(0, group, one, 0)

    @pl.when(step == pl.num_programs(0) - 1)
    def _():
        if last and halves == 2:
            keep_ref, send_ref = outs
            count = ky_count // 2
            mine = pl.multiple_of(me_ref[0] * count, 8)
            other = pl.multiple_of((1 - me_ref[0]) * count, 8)
            for part in range(2):
                keep_ref[part] = acc[part, pl.ds(mine, count), :]
                send_ref[part] = acc[part, pl.ds(other, count), :]
        else:
            outs[0][...] = acc[...]


def image_chunk(arrived, sensitivity, kz, ky, acc, me, group, lines, stride, first_unit, last, halves):
    sources, rows_all, packed = arrived.shape
    rows = group * lines
    units = rows_all // rows
    ky_count, kz_count = sensitivity.shape[-2:]
    half = kz.shape[1] // 2
    in_specs = [
        pl.BlockSpec((sources, rows, packed), lambda i, me: (0, i, 0)),
        pl.BlockSpec((2, group, 1, ky_count, kz_count), lambda i, me: (0, i + first_unit, 0, 0, 0)),
        pl.BlockSpec(kz.shape, lambda i, me: (0, 0)),
        pl.BlockSpec(ky.shape, lambda i, me: (0, 0)),
    ]
    operands = [arrived, sensitivity, kz, ky]
    if acc is not None:
        in_specs.append(pl.BlockSpec(acc.shape, lambda i, me: (0, 0, 0)))
        operands.append(acc)
    image_shape = (2, ky_count, kz_count)
    shapes = [(2, ky_count // 2, kz_count)] * 2 if last and halves == 2 else [image_shape]
    flops = 2 * units * (sources * rows * packed * 2 * half + group * ky_count * ky.shape[1] * 2 * half)
    return pl.pallas_call(
        functools.partial(image_kernel, group, lines, stride, acc is None, last, halves),
        out_shape=[jax.ShapeDtypeStruct(s, jnp.float32) for s in shapes],
        grid_spec=pltpu.PrefetchScalarGridSpec(
            num_scalar_prefetch=1,
            grid=(units,),
            in_specs=in_specs,
            out_specs=[pl.BlockSpec(s, lambda i, me: (0, 0, 0)) for s in shapes],
            scratch_shapes=[
                pltpu.VMEM((sources, rows, 2 * half), jnp.float32),
                pltpu.VMEM((group, 2 * sources * stride, 2 * half), jnp.bfloat16),
                pltpu.VMEM(image_shape, jnp.float32),
            ],
        ),
        compiler_params=pltpu.CompilerParams(vmem_limit_bytes=VMEM_BYTES),
        cost_estimate=pl.CostEstimate(
            flops=flops, bytes_accessed=units * sources * rows * packed * 4, transcendentals=0
        ),
        name="image_of_coils",
    )(me, *operands)


def on_device(kspace, sensitivity, sampled, pole_y, order_y, pole_z, order_z):
    _, coils, _, lines, kz_count = kspace.shape
    sources = lax.axis_size("ro")
    halves = lax.axis_size("coil")
    ky_count = lines * sources
    half = round_up(kz_count, LANES)
    stride = round_up(lines, 16)
    group = 16 // math.gcd(lines, 16)
    units = coils // group
    total = sum(PLAN)
    plan = PLAN if units % total == 0 else (1,)
    plan = [units // sum(plan) * p for p in plan]
    first_line = (lax.axis_index("ro") * lines).reshape(1).astype(jnp.int32)
    me = lax.axis_index("coil").reshape(1).astype(jnp.int32)
    kz = kz_table(kz_count, half)
    ky = ky_table(ky_count, sources, stride)
    params = (sampled, pole_y, order_y, pole_z, order_z)

    starts = [sum(plan[:i]) for i in range(len(plan))]
    sends = [filter_chunk(kspace, first_line, params, group, s, n) for s, n in zip(starts, plan)]
    acc = None
    arrived = []
    for i, send in enumerate(sends):
        if i >= 2:
            acc = image_chunk(
                arrived[i - 2], sensitivity, kz, ky, acc, me, group, lines, stride, starts[i - 2], False, halves
            )[0]
            send, acc = lax.optimization_barrier((send, acc))
        arrived.append(lax.all_to_all(send, "ro", split_axis=0, concat_axis=0, tiled=True))
    for i in range(max(len(plan) - 2, 0), len(plan)):
        last = i == len(plan) - 1
        result = image_chunk(
            arrived[i], sensitivity, kz, ky, acc, me, group, lines, stride, starts[i], last, halves
        )
        acc = result[0]
    if halves == 2:
        keep, give = result
        image = keep + lax.ppermute(give, "coil", [(0, 1), (1, 0)])
        return image[:, None]
    return lax.psum_scatter(acc, "coil", scatter_dimension=1, tiled=True)[:, None]


def solution(mesh):
    return jax.shard_map(
        on_device,
        mesh=mesh,
        in_specs=(
            P(None, "coil", None, "ro", None),
            P(None, "coil", "ro", None, None),
            P(),
            P(),
            P(),
            P(),
            P(),
        ),
        out_specs=P(None, "ro", "coil", None),
        check_vma=False,
    )
```

time: 754 us -> 487 us (0.65)
  waiting for transfers between devices: 492 us -> 240 us
  matrix products: 149 us -> 0 us
  Pallas kernels: 0 us -> 105 us
  starting transfers between devices: 7.72 us -> 79.1 us
  other arithmetic: 26.7 us -> 1.17 us
  between operations: 13.8 us -> 0.05 us
    all_to_all x1 -> x3, waiting for transfers between devices: 384 us -> 224 us  [on_device(): lax.all_to_all(send, 'ro', split_axis=0, concat_axis=0, tiled=True)]
    dot_general x8 -> x0, matrix products: 149 us -> none  [the longest x1 31.5 us: on_device(): jnp.einsum('nk,cakz->canz', ky_sine, hyb_real, preferred_element_type=jnp...]
    unnamed x2 -> x0, waiting for transfers between devices: 108 us -> none
    pallas_call x0 -> x6, Pallas kernels: none -> 105 us  [the longest x3 73.8 us: image_chunk(): pl.pallas_call(functools.partial(image_kernel, group, lines, stride, acc...]
    all_to_all x1 -> x3, starting transfers between devices: 7.39 us -> 77.6 us  [on_device(): lax.all_to_all(send, 'ro', split_axis=0, concat_axis=0, tiled=True)]
    unnamed x7 -> x4, local copies, waits for them, and re-layouts: 11.3 us -> 52.6 us
    another operation x2 -> x0, local copies, waits for them, and re-layouts: 31.7 us -> none
    convert_element_type x5 -> x0, other arithmetic: 18.9 us -> none  [the longest x1 17.3 us: on_device(): (kspace.astype(jnp.float32) * (weight_y * weight_z)).astype(jnp.bfloat16)]
  transfers between devices with their start and end apart: 2 -> 4, of which waited for: 2 -> 4; matrix products, arithmetic and copies ran while one was open for 0% -> 6% of each run, Pallas kernels for 0% -> 17%
where the time goes in v1:
time: 487 us; the launch traced here: 481 us
  waiting for transfers between devices  240 us (49%)
  Pallas kernels  105 us (22%)
  starting transfers between devices  79.1 us (16%)
  local copies, waits for them, and re-layouts  55.3 us (11%)
    all_to_all x3, waiting for transfers between devices, on_device(): lax.all_to_all(send, 'ro', split_axis=0, concat_axis=0, tiled=True)  224 us
    all_to_all x3, starting transfers between devices, on_device(): lax.all_to_all(send, 'ro', split_axis=0, concat_axis=0, tiled=True)  77.6 us
    pallas_call x3, Pallas kernels, image_chunk(): pl.pallas_call(functools.partial(image_kernel, group, lines, stride, acc...  73.8 us
    unnamed x4, local copies, waits for them, and re-layouts  52.6 us
    pallas_call x3, Pallas kernels, filter_chunk(): pl.pallas_call(functools.partial(filter_kernel, readouts, group, lines),...  31.3 us
    ppermute x1, waiting for transfers between devices, on_device(): image = keep + lax.ppermute(give, 'coil', [(0, 1), (1, 0)])  15.9 us
  transfers between devices with their start and end apart: 4, of which 4 were waited for; matrix products, arithmetic and copies ran while one was open for 6% of the time, Pallas kernels for 17%

profile of v1, /device:TPU:0, one launch (start us, length us, event | category | flops | bytes accessed | tf_op | source)
XLA Modules:
  0.0 480.7 jit_solution(11346409264305572947)
XLA Ops:
  0.0 23.2 %copy.17.x_ref = bf16[2,32,16,28,320]{4,3,2,1,0:T(8,128)(2,1)} copy(bf16[2,32,16,28,320]{4,2,3,1,0:T(8,128)(2,1)} %param.9) | data formatting | bytes 36700160 | tf_op args[0]
  23.2 11.2 %window_lines.4 = bf16[16,336,640]{2,1,0:T(8,128)(2,1)} custom-call(s32[1]{0:T(128)} %bitcast.1.first_ref, bf16[2,32,16,28,320]{4,3,2,1,0:T(8,128)(2,1)} %copy.17.x_ref, s32[16,448]{1,0:T(8,128)} %sampled_ref.5, s32[16,320]{1,0:T(8,128)} %pole_y_ref.5, s32[16,320]{1,0:T(8,128)} %order_y_ref.5, s32[16,448]{1,0:T(8,128)} %pole_z_ref.5, s32[16,448]{1,0:T(8,128)} %order_z_ref.5), custom_call_target="tpu_custom_call" | custom-call | bytes 17203200 | tf_op jit(solution)/shard_map/window_lines/pallas_call | solution.py:113
  34.4 7.4 %all-to-all-start = ((bf16[16,336,640]{2,1,0:T(8,128)(2,1)}), bf16[16,336,640]{2,1,0:T(8,128)(2,1)}, u32[]{:S(2)}, u32[]{:S(2)}) async-start(bf16[16,336,640]{2,1,0:T(8,128)(2,1)} %window_lines.4), calls=%async_computation | async-start | bytes 13762560 | tf_op jit(solution)/shard_map/all_to_all | solution.py:263
  41.9 13.8 %window_lines.5 = bf16[16,448,640]{2,1,0:T(8,128)(2,1)} custom-call(s32[1]{0:T(128)} %bitcast.1.first_ref, bf16[2,32,16,28,320]{4,3,2,1,0:T(8,128)(2,1)} %copy.17.x_ref, s32[16,448]{1,0:T(8,128)} %sampled_ref.5, s32[16,320]{1,0:T(8,128)} %pole_y_ref.5, s32[16,320]{1,0:T(8,128)} %order_y_ref.5, s32[16,448]{1,0:T(8,128)} %pole_z_ref.5, s32[16,448]{1,0:T(8,128)} %order_z_ref.5), custom_call_target="tpu_custom_call" | custom-call | bytes 22937600 | tf_op jit(solution)/shard_map/window_lines/pallas_call | solution.py:113
  55.6 110.7 %all-to-all-done.x_ref = bf16[16,336,640]{2,1,0:T(8,128)(2,1)} async-done(((bf16[16,336,640]{2,1,0:T(8,128)(2,1)}), bf16[16,336,640]{2,1,0:T(8,128)(2,1)}, u32[]{:S(2)}, u32[]{:S(2)}) %all-to-all-start) | async-done | bytes 6881312 | tf_op jit(solution)/shard_map/all_to_all | solution.py:263
  166.3 30.5 %all-to-all-start.2 = ((bf16[16,448,640]{2,1,0:T(8,128)(2,1)}), bf16[16,448,640]{2,1,0:T(8,128)(2,1)}, u32[]{:S(2)}, u32[]{:S(2)}) async-start(bf16[16,448,640]{2,1,0:T(8,128)(2,1)} %window_lines.5), calls=%async_computation.2 | async-start | bytes 18350080 | tf_op jit(solution)/shard_map/all_to_all | solution.py:263
  196.8 6.3 %window_lines.3 = bf16[16,112,640]{2,1,0:T(8,128)(2,1)} custom-call(s32[1]{0:T(128)} %bitcast.1.first_ref, bf16[2,32,16,28,320]{4,3,2,1,0:T(8,128)(2,1)} %copy.17.x_ref, s32[16,448]{1,0:T(8,128)} %sampled_ref.5, s32[16,320]{1,0:T(8,128)} %pole_y_ref.5, s32[16,320]{1,0:T(8,128)} %order_y_ref.5, s32[16,448]{1,0:T(8,128)} %pole_z_ref.5, s32[16,448]{1,0:T(8,128)} %order_z_ref.5), custom_call_target="tpu_custom_call" | custom-call | bytes 5734400 | tf_op jit(solution)/shard_map/window_lines/pallas_call | solution.py:113
  203.1 28.0 %copy.19.maps_ref = bf16[2,32,1,448,320]{4,3,2,1,0:T(8,128)(2,1)} copy(bf16[2,32,1,448,320]{3,4,2,1,0:T(8,128)(2,1)} %param.10) | data formatting | bytes 36700160 | tf_op args[1]
  231.1 26.7 %image_of_coils.3.refs_0_ = f32[2,448,320]{2,1,0:T(8,128)} custom-call(s32[1]{0:T(128)} %bitcast.me_ref, bf16[16,336,640]{2,1,0:T(8,128)(2,1)} %all-to-all-done.x_ref, bf16[2,32,1,448,320]{4,3,2,1,0:T(8,128)(2,1)} %copy.19.maps_ref, bf16[640,768]{1,0:T(8,128)(2,1)} %constant.15.clone.kz_ref, bf16[448,1024]{1,0:T(8,128)(2,1)} %constant.16.clone.ky_ref), custom_call_target="tpu_custom_call" | custom-call | flops 13740539904 | bytes 13762560 | tf_op jit(solution)/shard_map/image_of_coils/pallas_call | solution.py:213
  257.8 103.4 %all-to-all-done.2.x_ref = bf16[16,448,640]{2,1,0:T(8,128)(2,1)} async-done(((bf16[16,448,640]{2,1,0:T(8,128)(2,1)}), bf16[16,448,640]{2,1,0:T(8,128)(2,1)}, u32[]{:S(2)}, u32[]{:S(2)}) %all-to-all-start.2) | async-done | bytes 9175072 | tf_op jit(solution)/shard_map/all_to_all | solution.py:263
  361.2 39.7 %all-to-all-start.1 = ((bf16[16,112,640]{2,1,0:T(8,128)(2,1)}), bf16[16,112,640]{2,1,0:T(8,128)(2,1)S(1)}, u32[]{:S(2)}, u32[]{:S(2)}) async-start(bf16[16,112,640]{2,1,0:T(8,128)(2,1)} %window_lines.3), calls=%async_computation.1 | async-start | bytes 4587520 | tf_op jit(solution)/shard_map/all_to_all | solution.py:263
  400.9 34.6 %image_of_coils.4.refs_0_ = f32[2,448,320]{2,1,0:T(8,128)} custom-call(s32[1]{0:T(128)} %bitcast.me_ref, bf16[16,448,640]{2,1,0:T(8,128)(2,1)} %all-to-all-done.2.x_ref, bf16[2,32,1,448,320]{4,3,2,1,0:T(8,128)(2,1)} %copy.19.maps_ref, bf16[640,768]{1,0:T(8,128)(2,1)} %constant.15.clone.kz_ref, bf16[448,1024]{1,0:T(8,128)(2,1)} %constant.16.clone.ky_ref, ...), custom_call_target="tpu_custom_call" | custom-call | flops 18320719872 | bytes 18350080 | tf_op jit(solution)/shard_map/image_of_coils/pallas_call | solution.py:213
  435.5 9.9 %all-to-all-done.1.x_ref = bf16[16,112,640]{2,1,0:T(8,128)(2,1)S(1)} async-done(((bf16[16,112,640]{2,1,0:T(8,128)(2,1)}), bf16[16,112,640]{2,1,0:T(8,128)(2,1)S(1)}, u32[]{:S(2)}, u32[]{:S(2)}) %all-to-all-start.1) | async-done | bytes 2293792 | tf_op jit(solution)/shard_map/all_to_all | solution.py:263
  445.4 0.0 copy-start
  445.4 1.4 copy-done
  446.8 12.5 %image_of_coils.5 = (f32[2,224,320]{2,1,0:T(8,128)}, f32[2,224,320]{2,1,0:T(8,128)}) custom-call(s32[1]{0:T(128)} %bitcast.me_ref, bf16[16,112,640]{2,1,0:T(8,128)(2,1)} %copy-done, bf16[2,32,1,448,320]{4,3,2,1,0:T(8,128)(2,1)} %copy.19.maps_ref, bf16[640,768]{1,0:T(8,128)(2,1)} %constant.15.clone.kz_ref, bf16[448,1024]{1,0:T(8,128)(2,1)} %constant.16.clone.ky_ref, ...), custom_call_target="tpu_custom_call" | custom-call | flops 4580179968 | bytes 4587520 | tf_op jit(solution)/shard_map/image_of_coils/pallas_call | solution.py:213
  459.3 1.3 copy.23
  460.7 1.6 collective-permute-start
  462.3 15.9 %collective-permute-done = f32[2,224,320]{1,2,0:T(8,128)S(1)} collective-permute-done((f32[2,224,320]{1,2,0:T(8,128)S(1)}, f32[2,224,320]{1,2,0:T(8,128)S(1)}, u32[]{:S(2)}, u32[]{:S(2)}) %collective-permute-start) | collective-permute-done | bytes 573472 | tf_op jit(solution)/shard_map/ppermute | solution.py:272
  478.2 0.3 copy.24
  478.4 1.2 add_bitcast_fusion
  479.6 1.1 copy.25
Async XLA Ops:
  34.4 131.9 %all-to-all-start = ((bf16[16,336,640]{2,1,0:T(8,128)(2,1)}), bf16[16,336,640]{2,1,0:T(8,128)(2,1)}, u32[]{:S(2)}, u32[]{:S(2)}) async-start(bf16[16,336,640]{2,1,0:T(8,128)(2,1)} %window_lines.4), calls=%async_computation | async-start | bytes 13762560 | tf_op jit(solution)/shard_map/all_to_all | solution.py:263
  166.3 194.9 %all-to-all-start.2 = ((bf16[16,448,640]{2,1,0:T(8,128)(2,1)}), bf16[16,448,640]{2,1,0:T(8,128)(2,1)}, u32[]{:S(2)}, u32[]{:S(2)}) async-start(bf16[16,448,640]{2,1,0:T(8,128)(2,1)} %window_lines.5), calls=%async_computation.2 | async-start | bytes 18350080 | tf_op jit(solution)/shard_map/all_to_all | solution.py:263
  361.2 84.2 %all-to-all-start.1 = ((bf16[16,112,640]{2,1,0:T(8,128)(2,1)}), bf16[16,112,640]{2,1,0:T(8,128)(2,1)S(1)}, u32[]{:S(2)}, u32[]{:S(2)}) async-start(bf16[16,112,640]{2,1,0:T(8,128)(2,1)} %window_lines.3), calls=%async_computation.1 | async-start | bytes 4587520 | tf_op jit(solution)/shard_map/all_to_all | solution.py:263
  445.4 1.4 copy-start
  460.7 17.5 %collective-permute-start = (f32[2,224,320]{1,2,0:T(8,128)S(1)}, f32[2,224,320]{1,2,0:T(8,128)S(1)}, u32[]{:S(2)}, u32[]{:S(2)}) collective-permute-start(f32[2,224,320]{1,2,0:T(8,128)S(1)} %copy.23), channel_id=1, source_target_pairs={{0,16},{16,0},{1,17},{17,1},{2,18},{18,2},{3,19},{19,3},{4,20},{20... | collective-permute-start | bytes 1720328 | tf_op jit(solution)/shard_map/ppermute | solution.py:272

commit v2 on v1

v2 whole, which is shorter than its diff:
```python
import functools
import math

import jax
import jax.numpy as jnp
import ml_dtypes
import numpy as np
from jax import lax
from jax.experimental import pallas as pl
from jax.experimental.pallas import tpu as pltpu
from jax.sharding import PartitionSpec as P

LANES = 128
VMEM_BYTES = 56 * 2**20
PLAN = (1, 6, 1)


def round_up(value, step):
    return (value + step - 1) // step * step


def dft_tables(length):
    index = np.arange(length, dtype=np.int64)
    product = index[:, None] * index[None, :] % length
    angle = product.astype(np.float32) * np.float32(2.0 * math.pi / length)
    factor = np.float32(1.0 / math.sqrt(length))
    return (
        (np.cos(angle) * factor).astype(ml_dtypes.bfloat16).astype(np.float32),
        (np.sin(angle) * factor).astype(ml_dtypes.bfloat16).astype(np.float32),
    )


def kz_table(length):
    cosine, sine = dft_tables(length)
    table = np.block([[cosine, -sine], [sine, cosine]])
    return jnp.asarray(table.astype(ml_dtypes.bfloat16))


def ky_table(length, width, groups, stride):
    lines = length // groups

    def padded(part):
        table = np.zeros((groups, stride, width), np.float32)
        table[:, :lines, :length] = part.T.reshape(groups, lines, length)
        return table.reshape(groups * stride, width)

    cosine, sine = (padded(part) for part in dft_tables(length))
    table = np.block([[cosine, sine], [-sine, cosine]])
    return jnp.asarray(table.astype(ml_dtypes.bfloat16))


def growth(frequency, pole, order):
    quotient = frequency / pole
    square = quotient * quotient
    fourth = square * square
    return 1.0 + jnp.where(order < 1.5, square, jnp.where(order < 2.5, fourth, fourth * square))


def fold(index, length):
    return jnp.minimum(index, length - index).astype(jnp.float32)


def filter_kernel(
    first_ref, x_ref, sampled_ref, pole_y_ref, order_y_ref, pole_z_ref, order_z_ref, o_ref, weight, packed
):
    _, group, lines, readouts, kz_count = x_ref.shape
    ky_count = sampled_ref.shape[-1]
    rows = group * lines
    tiles = packed.shape[0]

    @pl.when(pl.program_id(0) == 0)
    def _():
        first = first_ref[0]
        width = round_up(lines, LANES)
        line = lax.broadcasted_iota(jnp.int32, (ky_count, width), 1) + first
        place = lax.broadcasted_iota(jnp.int32, (ky_count, width), 0)
        pick = (line == place).astype(jnp.bfloat16)

        def mine(ref):
            return jnp.dot(
                ref[...].astype(jnp.float32).astype(jnp.bfloat16), pick, preferred_element_type=jnp.float32
            )

        sampled, pole_z, order_z = mine(sampled_ref), mine(pole_z_ref), mine(order_z_ref)
        pole_y = pole_y_ref[...].astype(jnp.float32)
        order_y = order_y_ref[...].astype(jnp.float32)
        freq_z = fold(lax.broadcasted_iota(jnp.int32, (readouts, kz_count), 1), kz_count)
        for k in range(lines):
            freq_y = fold(jnp.full((readouts, kz_count), first + k, jnp.int32), ky_count)
            column_y = growth(freq_y, pole_y, order_y)
            column_z = growth(freq_z, pole_z[:, k : k + 1], order_z[:, k : k + 1])
            weight[k] = sampled[:, k : k + 1] / (column_y * column_z)

    def one(k, _):
        w = weight[k]
        for c in range(group):
            at = pl.ds(pl.multiple_of((c * lines + k) * readouts, 16), readouts)
            line = jnp.concatenate([x_ref[part, c, k].astype(jnp.float32) * w for part in range(2)], axis=1)
            for t in range(tiles):
                packed[t, at, :] = line[:, t * LANES : (t + 1) * LANES]
        return 0

    lax.fori_loop(0, lines, one, 0, unroll=2)
    for t in range(tiles):
        for r in range(readouts):
            o_ref[r, :, t * LANES : (t + 1) * LANES] = packed[t, pl.ds(r, rows, stride=readouts), :].astype(
                jnp.bfloat16
            )


def filter_chunk(lines_first, first_line, params, group, first_unit, units):
    _, _, lines, readouts, kz_count = lines_first.shape
    rows = group * lines
    whole = [pl.BlockSpec(p.shape, lambda i, first: (0, 0)) for p in params]
    return pl.pallas_call(
        filter_kernel,
        out_shape=jax.ShapeDtypeStruct((readouts, units * rows, 2 * kz_count), jnp.bfloat16),
        grid_spec=pltpu.PrefetchScalarGridSpec(
            num_scalar_prefetch=1,
            grid=(units,),
            in_specs=[
                pl.BlockSpec((2, group, lines, readouts, kz_count), lambda i, first: (0, i + first_unit, 0, 0, 0)),
                *whole,
            ],
            out_specs=pl.BlockSpec((readouts, rows, 2 * kz_count), lambda i, first: (0, i, 0)),
            scratch_shapes=[
                pltpu.VMEM((lines, readouts, kz_count), jnp.float32),
                pltpu.VMEM((2 * kz_count // LANES, rows * readouts, LANES), jnp.float32),
            ],
        ),
        compiler_params=pltpu.CompilerParams(vmem_limit_bytes=VMEM_BYTES),
        cost_estimate=pl.CostEstimate(
            flops=0, bytes_accessed=5 * units * readouts * rows * 2 * kz_count, transcendentals=0
        ),
        name="window_lines",
    )(first_line, lines_first, *params)


def image_kernel(fresh, last, halves, lines, me_ref, x_ref, maps_ref, kz_ref, ky_ref, *refs):
    refs = list(refs)
    acc_in = None if fresh else refs.pop(0)
    outs, (wide, by_coil, hybrid, acc) = refs[:-4], refs[-4:]
    sources = x_ref.shape[0]
    kz_count, ky_count = maps_ref.shape[-2:]
    group, depth, _ = by_coil.shape
    stride = depth // sources
    width = ky_ref.shape[1] // 2
    step = pl.program_id(0)

    @pl.when(step == 0)
    def _():
        acc[...] = jnp.zeros_like(acc) if fresh else acc_in[...]
        by_coil[...] = jnp.zeros_like(by_coil)

    def place(s, _):
        wide[...] = x_ref[s].astype(jnp.float32)
        base = pl.multiple_of(s * stride, stride)
        for c in range(group):
            by_coil[c, pl.ds(base, lines), :] = wide[pl.ds(lines * c, lines), :].astype(jnp.bfloat16)
        return 0

    lax.fori_loop(0, sources, place, 0)

    for c in range(group):
        mixed = lax.dot_general(
            kz_ref[...], by_coil[c], (((1,), (1,)), ((), ())), preferred_element_type=jnp.float32
        )
        hybrid[c, :, :depth] = mixed[:kz_count].astype(jnp.bfloat16)
        hybrid[c, :, depth:] = mixed[kz_count:].astype(jnp.bfloat16)
    for c in range(group):
        image = jnp.dot(hybrid[c], ky_ref[...], preferred_element_type=jnp.float32)
        real, imag = image[:, :ky_count], image[:, width : width + ky_count]
        map_real = maps_ref[0, c, 0].astype(jnp.float32)
        map_imag = maps_ref[1, c, 0].astype(jnp.float32)
        acc[0] += map_real * real + map_imag * imag
        acc[1] += map_real * imag - map_imag * real

    @pl.when(step == pl.num_programs(0) - 1)
    def _():
        if last and halves == 2:
            keep_ref, send_ref = outs
            count = ky_count // 2
            lower = me_ref[0] == 0
            for part in range(2):
                low, high = acc[part, :, :count], acc[part, :, count:]
                keep_ref[part] = jnp.where(lower, low, high)
                send_ref[part] = jnp.where(lower, high, low).astype(send_ref.dtype)
        else:
            outs[0][...] = acc[...]


def image_chunk(arrived, maps, kz, ky, acc, me, group, lines, stride, first_unit, last, halves):
    sources, rows_all, packed = arrived.shape
    rows = group * lines
    units = rows_all // rows
    kz_count, ky_count = maps.shape[-2:]
    depth = sources * stride
    in_specs = [
        pl.BlockSpec((sources, rows, packed), lambda i, me: (0, i, 0)),
        pl.BlockSpec((2, group, 1, kz_count, ky_count), lambda i, me: (0, i + first_unit, 0, 0, 0)),
        pl.BlockSpec(kz.shape, lambda i, me: (0, 0)),
        pl.BlockSpec(ky.shape, lambda i, me: (0, 0)),
    ]
    operands = [arrived, maps, kz, ky]
    if acc is not None:
        in_specs.append(pl.BlockSpec(acc.shape, lambda i, me: (0, 0, 0)))
        operands.append(acc)
    image_shape = (2, kz_count, ky_count)
    outs = [jax.ShapeDtypeStruct(image_shape, jnp.float32)]
    if last and halves == 2:
        half_shape = (2, kz_count, ky_count // 2)
        outs = [jax.ShapeDtypeStruct(half_shape, jnp.float32), jax.ShapeDtypeStruct(half_shape, jnp.bfloat16)]
    flops = 2 * units * group * (packed * packed * depth + kz_count * ky.shape[0] * ky.shape[1])
    return pl.pallas_call(
        functools.partial(image_kernel, acc is None, last, halves, lines),
        out_shape=outs,
        grid_spec=pltpu.PrefetchScalarGridSpec(
            num_scalar_prefetch=1,
            grid=(units,),
            in_specs=in_specs,
            out_specs=[pl.BlockSpec(o.shape, lambda i, me: (0, 0, 0)) for o in outs],
            scratch_shapes=[
                pltpu.VMEM((rows, packed), jnp.float32),
                pltpu.VMEM((group, depth, packed), jnp.bfloat16),
                pltpu.VMEM((group, kz_count, 2 * depth), jnp.bfloat16),
                pltpu.VMEM(image_shape, jnp.float32),
            ],
        ),
        compiler_params=pltpu.CompilerParams(vmem_limit_bytes=VMEM_BYTES),
        cost_estimate=pl.CostEstimate(
            flops=flops, bytes_accessed=units * sources * rows * packed * 4, transcendentals=0
        ),
        name="image_of_coils",
    )(me, *operands)


def on_device(kspace, sensitivity, sampled, pole_y, order_y, pole_z, order_z):
    _, coils, _, lines, kz_count = kspace.shape
    sources = lax.axis_size("ro")
    halves = lax.axis_size("coil")
    ky_count = lines * sources
    stride = round_up(lines, 16)
    group = 16 // math.gcd(lines, 16)
    units = coils // group
    total = sum(PLAN)
    plan = PLAN if units % total == 0 else (1,)
    plan = [units // sum(plan) * p for p in plan]
    first_line = (lax.axis_index("ro") * lines).reshape(1).astype(jnp.int32)
    me = lax.axis_index("coil").reshape(1).astype(jnp.int32)
    kz = kz_table(kz_count)
    ky = ky_table(ky_count, round_up(ky_count, LANES), sources, stride)
    lines_first = jnp.swapaxes(kspace, 2, 3)
    maps = jnp.swapaxes(sensitivity, 3, 4)
    params = (sampled, pole_y, order_y, pole_z, order_z)

    starts = [sum(plan[:i]) for i in range(len(plan))]
    sends = [filter_chunk(lines_first, first_line, params, group, s, n) for s, n in zip(starts, plan)]
    acc = None
    arrived = []
    for i, send in enumerate(sends):
        if i >= 2:
            acc = image_chunk(
                arrived[i - 2], maps, kz, ky, acc, me, group, lines, stride, starts[i - 2], False, halves
            )[0]
            send, acc = lax.optimization_barrier((send, acc))
        arrived.append(lax.all_to_all(send, "ro", split_axis=0, concat_axis=0, tiled=True))
    for i in range(max(len(plan) - 2, 0), len(plan)):
        last = i == len(plan) - 1
        result = image_chunk(
            arrived[i], maps, kz, ky, acc, me, group, lines, stride, starts[i], last, halves
        )
        acc = result[0]
    if halves == 2:
        keep, give = result
        image = keep + lax.ppermute(give, "coil", [(0, 1), (1, 0)]).astype(jnp.float32)
    else:
        image = lax.psum_scatter(acc, "coil", scatter_dimension=2, tiled=True)
    return jnp.swapaxes(image, 1, 2)[:, None]


def solution(mesh):
    return jax.shard_map(
        on_device,
        mesh=mesh,
        in_specs=(
            P(None, "coil", None, "ro", None),
            P(None, "coil", "ro", None, None),
            P(),
            P(),
            P(),
            P(),
            P(),
        ),
        out_specs=P(None, "ro", "coil", None),
        check_vma=False,
    )
```

time: 487 us -> 451 us (0.926)
  local copies, waits for them, and re-layouts: 55.3 us -> 2.76 us
  waiting for transfers between devices: 240 us -> 259 us
    unnamed x4, local copies, waits for them, and re-layouts: 52.6 us -> 2.76 us
    all_to_all x3, waiting for transfers between devices: 224 us -> 250 us  [on_device(): lax.all_to_all(send, 'ro', split_axis=0, concat_axis=0, tiled=True)]
    ppermute x1, waiting for transfers between devices: 15.9 us -> 9.11 us  [on_device(): lax.ppermute(give, 'coil', [(0, 1), (1, 0)]).astype(jnp.float32)]
  transfers between devices with their start and end apart: 4 -> 4, of which waited for: 4 -> 4; matrix products, arithmetic and copies ran while one was open for 6% -> 0% of each run, Pallas kernels for 17% -> 19%
where the time goes in v2:
time: 451 us; the launch traced here: 445 us
  waiting for transfers between devices  259 us (57%)
  Pallas kernels  102 us (23%)
  starting transfers between devices  79 us (18%)
    all_to_all x3, waiting for transfers between devices, on_device(): lax.all_to_all(send, 'ro', split_axis=0, concat_axis=0, tiled=True)  250 us
    all_to_all x3, starting transfers between devices, on_device(): lax.all_to_all(send, 'ro', split_axis=0, concat_axis=0, tiled=True)  77.5 us
    pallas_call x3, Pallas kernels, image_chunk(): pl.pallas_call(functools.partial(image_kernel, acc is None, last, halves,...  64.3 us
    pallas_call x3, Pallas kernels, filter_chunk(): pl.pallas_call(filter_kernel, out_shape=jax.ShapeDtypeStruct((readouts, u...  37.7 us
    ppermute x1, waiting for transfers between devices, on_device(): lax.ppermute(give, 'coil', [(0, 1), (1, 0)]).astype(jnp.float32)  9.11 us
  transfers between devices with their start and end apart: 4, of which 4 were waited for; matrix products, arithmetic and copies ran while one was open for 0% of the time, Pallas kernels for 19%

profile of v2, /device:TPU:0, one launch (start us, length us, event | category | flops | bytes accessed | tf_op | source)
XLA Modules:
  0.0 444.8 jit_solution(16006847433279441849)
XLA Ops:
  0.0 7.1 %window_lines.4 = bf16[16,112,640]{2,1,0:T(8,128)(2,1)} custom-call(s32[1]{0:T(128)} %bitcast.1.first_ref, bf16[2,32,28,16,320]{4,3,2,1,0:T(8,128)(2,1)} %bitcast.10, s32[16,448]{1,0:T(8,128)} %sampled_ref.5, s32[16,320]{1,0:T(8,128)} %pole_y_ref.5, s32[16,320]{1,0:T(8,128)} %order_y_ref.5, s32[16,448]{1,0:T(8,128)} %pole_z_ref.5, s32[16,448]{1,0:T(8,128)} %order_z_ref.5), custom_call_target="tpu_custom_call" | custom-call | bytes 5734400 | tf_op jit(solution)/shard_map/window_lines/pallas_call | solution.py:115
  7.1 7.4 %all-to-all-start = ((bf16[16,112,640]{2,1,0:T(8,128)(2,1)}), bf16[16,112,640]{2,1,0:T(8,128)(2,1)S(1)}, u32[]{:S(2)}, u32[]{:S(2)}) async-start(bf16[16,112,640]{2,1,0:T(8,128)(2,1)} %window_lines.4), calls=%async_computation | async-start | bytes 4587520 | tf_op jit(solution)/shard_map/all_to_all | solution.py:266
  14.5 23.4 %window_lines.5 = bf16[16,672,640]{2,1,0:T(8,128)(2,1)} custom-call(s32[1]{0:T(128)} %bitcast.1.first_ref, bf16[2,32,28,16,320]{4,3,2,1,0:T(8,128)(2,1)} %bitcast.11, s32[16,448]{1,0:T(8,128)} %sampled_ref.5, s32[16,320]{1,0:T(8,128)} %pole_y_ref.5, s32[16,320]{1,0:T(8,128)} %order_y_ref.5, s32[16,448]{1,0:T(8,128)} %pole_z_ref.5, s32[16,448]{1,0:T(8,128)} %order_z_ref.5), custom_call_target="tpu_custom_call" | custom-call | bytes 34406400 | tf_op jit(solution)/shard_map/window_lines/pallas_call | solution.py:115
  37.9 21.2 %all-to-all-done.x_ref = bf16[16,112,640]{2,1,0:T(8,128)(2,1)S(1)} async-done(((bf16[16,112,640]{2,1,0:T(8,128)(2,1)}), bf16[16,112,640]{2,1,0:T(8,128)(2,1)S(1)}, u32[]{:S(2)}, u32[]{:S(2)}) %all-to-all-start) | async-done | bytes 2293792 | tf_op jit(solution)/shard_map/all_to_all | solution.py:266
  59.1 0.0 copy-start
  59.1 1.4 copy-done
  60.4 12.1 %all-to-all-start.2 = ((bf16[16,672,640]{2,1,0:T(8,128)(2,1)}), bf16[16,672,640]{2,1,0:T(8,128)(2,1)}, u32[]{:S(2)}, u32[]{:S(2)}) async-start(bf16[16,672,640]{2,1,0:T(8,128)(2,1)} %window_lines.5), calls=%async_computation.2 | async-start | bytes 27525120 | tf_op jit(solution)/shard_map/all_to_all | solution.py:266
  72.5 7.2 %window_lines.3 = bf16[16,112,640]{2,1,0:T(8,128)(2,1)} custom-call(s32[1]{0:T(128)} %bitcast.1.first_ref, bf16[2,32,28,16,320]{4,3,2,1,0:T(8,128)(2,1)} %bitcast.12, s32[16,448]{1,0:T(8,128)} %sampled_ref.5, s32[16,320]{1,0:T(8,128)} %pole_y_ref.5, s32[16,320]{1,0:T(8,128)} %order_y_ref.5, s32[16,448]{1,0:T(8,128)} %pole_z_ref.5, s32[16,448]{1,0:T(8,128)} %order_z_ref.5), custom_call_target="tpu_custom_call" | custom-call | bytes 5734400 | tf_op jit(solution)/shard_map/window_lines/pallas_call | solution.py:115
  79.7 10.9 %image_of_coils.3.refs_0_ = f32[2,320,448]{2,1,0:T(8,128)} custom-call(s32[1]{0:T(128)} %bitcast.me_ref, bf16[16,112,640]{2,1,0:T(8,128)(2,1)} %copy-done, bf16[2,32,1,320,448]{4,3,2,1,0:T(8,128)(2,1)} %bitcast.13, bf16[640,640]{1,0:T(8,128)(2,1)} %constant.15.clone.kz_ref, bf16[1024,1024]{1,0:T(8,128)(2,1)} %constant.16.clone.ky_ref), custom_call_target="tpu_custom_call" | custom-call | flops 4362076160 | bytes 4587520 | tf_op jit(solution)/shard_map/image_of_coils/pallas_call | solution.py:214
  90.6 226.2 %all-to-all-done.2.x_ref = bf16[16,672,640]{2,1,0:T(8,128)(2,1)} async-done(((bf16[16,672,640]{2,1,0:T(8,128)(2,1)}), bf16[16,672,640]{2,1,0:T(8,128)(2,1)}, u32[]{:S(2)}, u32[]{:S(2)}) %all-to-all-start.2) | async-done | bytes 13762592 | tf_op jit(solution)/shard_map/all_to_all | solution.py:266
  316.8 58.1 %all-to-all-start.1 = ((bf16[16,112,640]{2,1,0:T(8,128)(2,1)}), bf16[16,112,640]{2,1,0:T(8,128)(2,1)S(1)}, u32[]{:S(2)}, u32[]{:S(2)}) async-start(bf16[16,112,640]{2,1,0:T(8,128)(2,1)} %window_lines.3), calls=%async_computation.1 | async-start | bytes 4587520 | tf_op jit(solution)/shard_map/all_to_all | solution.py:266
  374.9 42.0 %image_of_coils.4.refs_0_ = f32[2,320,448]{2,1,0:T(8,128)} custom-call(s32[1]{0:T(128)} %bitcast.me_ref, bf16[16,672,640]{2,1,0:T(8,128)(2,1)} %all-to-all-done.2.x_ref, bf16[2,32,1,320,448]{4,3,2,1,0:T(8,128)(2,1)} %bitcast.14, bf16[640,640]{1,0:T(8,128)(2,1)} %constant.15.clone.kz_ref, bf16[1024,1024]{1,0:T(8,128)(2,1)} %constant.16.clone.ky_ref, ...), custom_call_target="tpu_custom_call" | custom-call | flops 26172456960 | bytes 27525120 | tf_op jit(solution)/shard_map/image_of_coils/pallas_call | solution.py:214
  416.8 2.6 all-to-all-done.1.x_ref
  419.4 0.0 copy-start.1
  419.4 1.4 copy-done.1
  420.8 11.4 %image_of_coils.5 = (f32[2,320,224]{2,1,0:T(8,128)}, bf16[2,320,224]{2,1,0:T(8,128)(2,1)}) custom-call(s32[1]{0:T(128)} %bitcast.me_ref, bf16[16,112,640]{2,1,0:T(8,128)(2,1)} %copy-done.1, bf16[2,32,1,320,448]{4,3,2,1,0:T(8,128)(2,1)} %bitcast.15, bf16[640,640]{1,0:T(8,128)(2,1)} %constant.15.clone.kz_ref, bf16[1024,1024]{1,0:T(8,128)(2,1)} %constant.16.clone.ky_ref, ...), custom_call_target="tpu_custom_call" | custom-call | flops 4362076160 | bytes 4587520 | tf_op jit(solution)/shard_map/image_of_coils/pallas_call | solution.py:214
  432.2 1.5 collective-permute-start
  433.7 9.1 %collective-permute-done = bf16[2,320,224]{2,1,0:T(8,128)(2,1)S(1)} collective-permute-done((bf16[2,320,224]{2,1,0:T(8,128)(2,1)}, bf16[2,320,224]{2,1,0:T(8,128)(2,1)S(1)}, u32[]{:S(2)}, u32[]{:S(2)}) %collective-permute-start) | collective-permute-done | bytes 286752 | tf_op jit(solution)/shard_map/ppermute | solution.py:275
  442.8 2.0 add_bitcast_fusion
Async XLA Ops:
  7.1 51.9 %all-to-all-start = ((bf16[16,112,640]{2,1,0:T(8,128)(2,1)}), bf16[16,112,640]{2,1,0:T(8,128)(2,1)S(1)}, u32[]{:S(2)}, u32[]{:S(2)}) async-start(bf16[16,112,640]{2,1,0:T(8,128)(2,1)} %window_lines.4), calls=%async_computation | async-start | bytes 4587520 | tf_op jit(solution)/shard_map/all_to_all | solution.py:266
  59.1 1.4 copy-start
  60.4 256.3 %all-to-all-start.2 = ((bf16[16,672,640]{2,1,0:T(8,128)(2,1)}), bf16[16,672,640]{2,1,0:T(8,128)(2,1)}, u32[]{:S(2)}, u32[]{:S(2)}) async-start(bf16[16,672,640]{2,1,0:T(8,128)(2,1)} %window_lines.5), calls=%async_computation.2 | async-start | bytes 27525120 | tf_op jit(solution)/shard_map/all_to_all | solution.py:266
  316.8 102.6 %all-to-all-start.1 = ((bf16[16,112,640]{2,1,0:T(8,128)(2,1)}), bf16[16,112,640]{2,1,0:T(8,128)(2,1)S(1)}, u32[]{:S(2)}, u32[]{:S(2)}) async-start(bf16[16,112,640]{2,1,0:T(8,128)(2,1)} %window_lines.3), calls=%async_computation.1 | async-start | bytes 4587520 | tf_op jit(solution)/shard_map/all_to_all | solution.py:266
  419.4 1.4 copy-start.1
  432.2 10.6 %collective-permute-start = (bf16[2,320,224]{2,1,0:T(8,128)(2,1)}, bf16[2,320,224]{2,1,0:T(8,128)(2,1)S(1)}, u32[]{:S(2)}, u32[]{:S(2)}) collective-permute-start(bf16[2,320,224]{2,1,0:T(8,128)(2,1)} %get-tuple-element.12), channel_id=1, source_target_pairs={{0,16},{16,0},{1,17},{17,1},{2,18},{18,2},{3,19},{19,3},{4,20},{20... | collective-permute-start | bytes 860168 | tf_op jit(solution)/shard_map/ppermute | solution.py:275
